TPU v7x, 32 devices: a whole 2x2x4 slice. The times are simulated.
32 devices in a mesh: grp: 2 (over y), row: 4 (over z), col: 2 (over x), rep: 2 (over core).
Axes of the slice: x: 2, y: 2, z: 4, core: 2. Of those that a mesh axis runs over, the one named last changes fastest.
Arguments:
- features: bfloat16 [64, 65536], P(('grp', 'row'), ('col', 'rep')), parts along dimension 0, may hold values from 0 to 1
- tiles: bfloat16 [2, 4, 128, 4, 3, 128, 128], P(None, None, 'row', ('col', 'rep')), may hold values from -0.29882812 to 0.29882812
- tile_rows: int32 [2, 4, 128, 4, 3], P(None, None, 'row', ('col', 'rep')), may hold values from 0 to 127
- tile_counts: int32 [2, 4, 128, 4], P(None, None, 'row', ('col', 'rep')), may hold values from 0 to 3, as said below
- bias: float32 [2, 65536], P(None, ('col', 'rep')), may hold values from -0.3 to 0.3
Outputs:
- activations: bfloat16 [64, 65536], P(('grp', 'row'), ('col', 'rep')), parts along dimension 0
There are 2 independent parts, one for each index of `grp`. A program takes and returns all parts, laid end to end along the dimension named above; an argument that names none is the same for every part. Nothing has to cross between parts.
Inputs may be any that keep to these rules, and one draw needn't show every extreme that they name: `tile_counts`: in every layer each block column has exactly 3 live slots in one input piece and fewer in the others.
All inputs are finite; a program needn't handle non-finite values.
Results may differ from a plain program's by a relative error of at most 0.005.
Values may be sent and summed in bfloat16 or wider, within the bound.
A program may use at most 128 MiB of HBM per device.

v0:
```python
import jax
import jax.numpy as jnp
from jax import lax
from jax.sharding import PartitionSpec as P


def partial_products(rows_x, tiles, tile_rows, tile_counts, layer):
    tile_width = tiles.shape[-1]
    out_count = tiles.shape[1] * tiles.shape[2]
    slots = tiles.shape[4]
    height = rows_x.shape[0]
    blocks = rows_x.reshape(height, -1, tile_width)
    picks = tile_rows[layer].reshape(-1)
    picked = jnp.take(blocks, picks, axis=1)
    live = lax.broadcasted_iota(jnp.int32, (out_count, slots), 1) < tile_counts[layer].reshape(
        out_count, 1
    )
    picked = (
        picked.reshape(height, out_count, slots, tile_width)
        * live.astype(jnp.bfloat16)[None, :, :, None]
    )
    weights = tiles[layer].reshape(out_count, slots, tile_width, tile_width)
    summed = jnp.einsum("rosd,osde->roe", picked, weights, preferred_element_type=jnp.float32)
    return summed.reshape(height, out_count * tile_width)


def finish(summed, bias, layer):
    partial_value = lax.psum_scatter(summed, ("col", "rep"), scatter_dimension=1, tiled=True)
    width = partial_value.shape[1]
    offset = lax.axis_index("row") * width
    shifts = lax.dynamic_slice_in_dim(bias[layer], offset, width)
    return jax.nn.relu(partial_value + shifts[None, :]).astype(jnp.bfloat16)


def from_rows(current, tiles, tile_rows, tile_counts, layer):
    return partial_products(
        lax.all_gather(current, "row", axis=0, tiled=True), tiles, tile_rows, tile_counts, layer
    )


def relayout(finished):
    return lax.all_to_all(finished, "row", split_axis=0, concat_axis=1, tiled=True)


def on_device(features, tiles, tile_rows, tile_counts, bias):
    layers = tiles.shape[0]
    result = features
    for layer in range(layers):
        result = relayout(
            finish(from_rows(result, tiles, tile_rows, tile_counts, layer), bias, layer)
        )
    return result


def solution(mesh):
    in_specs = (
        P(("grp", "row"), ("col", "rep")),
        P(None, None, "row", ("col", "rep"), None, None, None),
        P(None, None, "row", ("col", "rep"), None),
        P(None, None, "row", ("col", "rep")),
        P(None, ("col", "rep")),
    )
    out_specs = P(("grp", "row"), ("col", "rep"))
    return jax.shard_map(
        on_device, mesh=mesh, in_specs=in_specs, out_specs=out_specs, check_vma=False
    )
```

profile of v0, /device:TPU:0, one launch (start us, length us, event | category | flops | bytes accessed | tf_op | source)
XLA Modules:
  0.0 193.5 jit_solution(341785708305455710)
XLA Ops:
  6.5 0.7 all-gather.3.cloned.1.call-update
  7.3 0.7 fusion.18
  8.1 0.2 reshape_squeeze.14
  8.4 0.7 slice_reduce_fusion
  9.3 20.9 %fusion.16 = (bf16[1,4,32,1,3,128,128]{6,5,4,3,2,1,0:T(8,128)(2,1)}, bf16[1,4,32,1,3,128,128]{6,5,4,3,2,1,0:T(8,128)(2,1)}) fusion(bf16[2,4,32,1,3,128,128]{6,5,4,3,2,1,0:T(8,128)(2,1)} %param.8), kind=kLoop, calls=%fused_computation.34 | loop fusion | bytes 50331648 | tf_op jit(solution)/shard_map/slice | solution.py:22
  30.2 9.4 %all-gather.3.cloned.1.call-done = bf16[32,16384]{1,0:T(8,128)(2,1)} async-done(((bf16[8,16384]{1,0:T(8,128)(2,1)}), bf16[32,16384]{1,0:T(8,128)(2,1)}) %all-gather.3.cloned.1.call-update) | async-done | bytes 1048592 | tf_op jit(solution)/shard_map/all_gather | solution.py:37
  39.6 1.4 copy_bitcast_fusion.3
  41.0 3.2 %gather_fusion = bf16[384,32,128]{2,1,0:T(8,128)(2,1)} fusion(bf16[32,128,128]{2,0,1:T(8,128)(2,1)S(1)} %copy_bitcast_fusion.3, s32[1024]{0:T(1024)S(1)} %pad_clamp_fusion.1), kind=kCustom, calls=%fused_computation.clone | custom fusion | bytes 6292992 | tf_op jit(solution)/shard_map/jit(_take)/gather | solution.py:14
  44.2 2.7 %broadcast_select_fusion.1 = bf16[384,32,128]{2,1,0:T(8,128)(2,1)S(1)} fusion(bf16[384,32,128]{2,1,0:T(8,128)(2,1)} %gather_fusion, pred[384]{0:T(512)(128)(4,1)S(1)} %compare_and_fusion.1), kind=kLoop, calls=%fused_computation.7 | loop fusion | flops 1572864 | bytes 6291840 | tf_op jit(solution)/shard_map/jit(_take)/select_n | solution.py:14
  46.9 5.9 %fusion.4 = f32[128,4,8,128]{3,2,1,0:T(8,128)S(1)} fusion(bf16[128,3,128,128]{3,2,1,0:T(8,128)(2,1)} %bitcast.59, bf16[32,128,3,128]{3,0,2,1:T(8,128)(2,1)S(1)} %bitcast.61, bf16[128,3]{1,0:T(8,128)(2,1)S(1)} %fusion.14), kind=kOutput, calls=%fused_computation.10 | convolution fusion | flops 404226048 | bytes 17826560 | tf_op jit(solution)/shard_map/rosd,osde->roe/dot_general | solution.py:23
  52.9 1.5 copy.28
  54.5 30.9 %reduce-scatter.3.cloned.1.call-done = f32[32,4096]{1,0:T(8,128)} async-done(((f32[32,16384]{1,0:T(8,128)}), f32[32,4096]{1,0:T(8,128)}) %reduce-scatter.3.cloned.1.call-update) | async-done | bytes 524304 | tf_op jit(solution)/shard_map/reduce_scatter | solution.py:28
  85.4 1.1 fusion.12
  86.5 13.4 %all_to_all.38 = bf16[4,8,4096]{2,1,0:T(8,128)(2,1)} all-to-all(bf16[4,8,4096]{2,1,0:T(8,128)(2,1)S(1)} %fusion.12), channel_id=1, replica_groups=mesh['grp'=2,'row'=4,'col'=2,'rep'=2] {'row'}, dimensions={0} | all-to-all | bytes 524288 | tf_op jit(solution)/shard_map/all_to_all | solution.py:42
  100.5 25.7 %all-gather.5.cloned.1.call-done = bf16[32,16384]{1,0:T(8,128)(2,1)} async-done(((bf16[8,16384]{1,0:T(8,128)(2,1)}), bf16[32,16384]{1,0:T(8,128)(2,1)}) %all-gather.5.cloned.1.call-update) | async-done | bytes 1048592 | tf_op jit(solution)/shard_map/all_gather | solution.py:37
  126.1 1.4 copy_bitcast_fusion.2
  127.5 3.1 %gather_fusion.1 = bf16[384,32,128]{2,1,0:T(8,128)(2,1)} fusion(bf16[32,128,128]{2,0,1:T(8,128)(2,1)S(1)} %copy_bitcast_fusion.2, s32[1024]{0:T(1024)S(1)} %pad_clamp_fusion), kind=kCustom, calls=%fused_computation.1.clone | custom fusion | bytes 6292992 | tf_op jit(solution)/shard_map/jit(_take)/gather | solution.py:14
  130.7 2.7 %broadcast_select_fusion = bf16[384,32,128]{2,1,0:T(8,128)(2,1)S(1)} fusion(bf16[384,32,128]{2,1,0:T(8,128)(2,1)} %gather_fusion.1, pred[384]{0:T(512)(128)(4,1)S(1)} %compare_and_fusion), kind=kLoop, calls=%fused_computation.6 | loop fusion | flops 1572864 | bytes 6291840 | tf_op jit(solution)/shard_map/jit(_take)/select_n | solution.py:14
  133.4 5.9 %fusion.7 = f32[128,4,8,128]{3,2,1,0:T(8,128)S(1)} fusion(bf16[128,3,128,128]{3,2,1,0:T(8,128)(2,1)} %bitcast.58, bf16[32,128,3,128]{3,0,2,1:T(8,128)(2,1)S(1)} %bitcast.60, bf16[128,3]{1,0:T(8,128)(2,1)S(1)} %fusion.15), kind=kOutput, calls=%fused_computation.11 | convolution fusion | flops 404226048 | bytes 17826560 | tf_op jit(solution)/shard_map/rosd,osde->roe/dot_general | solution.py:23
  139.3 1.5 copy.27
  140.8 31.1 %reduce-scatter.5.cloned.1.call-done = f32[32,4096]{1,0:T(8,128)} async-done(((f32[32,16384]{1,0:T(8,128)}), f32[32,4096]{1,0:T(8,128)}) %reduce-scatter.5.cloned.1.call-update) | async-done | bytes 524304 | tf_op jit(solution)/shard_map/reduce_scatter | solution.py:28
  171.9 1.1 fusion.13
  173.0 13.3 %all_to_all.39 = bf16[4,8,4096]{2,1,0:T(8,128)(2,1)S(1)} all-to-all(bf16[4,8,4096]{2,1,0:T(8,128)(2,1)S(1)} %fusion.13), channel_id=1, replica_groups=mesh['grp'=2,'row'=4,'col'=2,'rep'=2] {'row'}, dimensions={0} | all-to-all | bytes 524288 | tf_op jit(solution)/shard_map/all_to_all | solution.py:42
  186.3 0.7 copy.30
  (25 shorter events, 1.1 us)
Async XLA Ops:
  6.5 33.1 %all-gather.3.cloned.1.call-start = ((), (), s32[]{:S(2)}) async-start(), calls=%async_computation.4 | async-start | bytes 1310720 | tf_op jit(solution)/shard_map/all_gather | solution.py:37
  7.3 78.2 %reduce-scatter.3.cloned.1.call-start = ((), (), s32[]{:S(2)}) async-start(), calls=%async_computation.5 | async-start | bytes 2621440 | tf_op jit(solution)/shard_map/reduce_scatter | solution.py:28
  52.8 1.6 copy-start
  54.4 71.8 %all-gather.5.cloned.1.call-start = ((), (), s32[]{:S(2)}) async-start(), calls=%async_computation.6 | async-start | bytes 1310720 | tf_op jit(solution)/shard_map/all_gather | solution.py:37
  99.9 72.0 %reduce-scatter.5.cloned.1.call-start = ((), (), s32[]{:S(2)}) async-start(), calls=%async_computation.7 | async-start | bytes 2621440 | tf_op jit(solution)/shard_map/reduce_scatter | solution.py:28
Sparse Core Ops, SparseCore 0:
  8.9 30.6 all-gather.2
  54.5 30.9 reduce-scatter.2
  100.0 26.0 all-gather.4
  140.9 30.9 reduce-scatter.4
where the time goes:
time: 194 us; the launch traced here: 193 us
  waiting for transfers between devices  97.8 us (50%)
  local copies, waits for them, and re-layouts  36.1 us (19%)
  blocking collectives  26.6 us (14%)
  between operations  13.3 us (7%)
  matrix products  11.8 us (6%)
  other arithmetic  7.77 us (4%)
    reduce_scatter x2, waiting for transfers between devices, finish(): lax.psum_scatter(summed, ('col', 'rep'), scatter_dimension=1, tiled=True)  61.9 us
    all_gather x2, waiting for transfers between devices, from_rows(): lax.all_gather(current, 'row', axis=0, tiled=True)  35.1 us
    all_to_all x2, blocking collectives, relayout(): lax.all_to_all(finished, 'row', split_axis=0, concat_axis=1, tiled=True)  26.6 us
    slice x1, local copies, waits for them, and re-layouts, partial_products(): weights = tiles[layer].reshape(out_count, slots, tile_width, tile_width)  20.9 us
    dot_general x2, matrix products, partial_products(): jnp.einsum('rosd,osde->roe', picked, weights, preferred_element_type=jnp....  11.8 us
    gather x2, local copies, waits for them, and re-layouts, partial_products(): picked = jnp.take(blocks, picks, axis=1)  6.38 us
    select_n x4, other arithmetic, partial_products(): picked = jnp.take(blocks, picks, axis=1)  5.4 us
  transfers between devices with their start and end apart: 4, of which 4 were waited for; matrix products, arithmetic and copies ran while one was open for 12% of the time, Pallas kernels for 0%

commit v1 on v0

--- a/solution.py
+++ b/solution.py
@@ -1,7 +1,14 @@
+import functools
+
 import jax
 import jax.numpy as jnp
 from jax import lax
+from jax.experimental import pallas as pl
+from jax.experimental.pallas import tpu as pltpu
 from jax.sharding import PartitionSpec as P
+
+MESH = pl.DeviceIdType.MESH
+PARTS = 4
 
 
 def partial_products(rows_x, tiles, tile_rows, tile_counts, layer):
@@ -32,24 +39,361 @@
     return jax.nn.relu(partial_value + shifts[None, :]).astype(jnp.bfloat16)
 
 
-def from_rows(current, tiles, tile_rows, tile_counts, layer):
-    return partial_products(
-        lax.all_gather(current, "row", axis=0, tiled=True), tiles, tile_rows, tile_counts, layer
-    )
-
-
-def relayout(finished):
+def in_operations(features, tiles, tile_rows, tile_counts, bias):
+    layers = tiles.shape[0]
+    rows_x = lax.all_gather(features, "row", axis=0, tiled=True)
+    for layer in range(layers):
+        finished = finish(partial_products(rows_x, tiles, tile_rows, tile_counts, layer), bias, layer)
+        if layer + 1 < layers:
+            rows_x = lax.all_gather(finished, "row", axis=1, tiled=True)
     return lax.all_to_all(finished, "row", split_axis=0, concat_axis=1, tiled=True)
 
 
-def on_device(features, tiles, tile_rows, tile_counts, bias):
-    layers = tiles.shape[0]
-    result = features
+class Chain:
+    def __init__(self, count, place, sems):
+        self.count, self.place, self.sems = count, place, sems
+        self.me = lax.axis_index("row")
+
+    def copy(self, way, hop, part):
+        step = 1 - 2 * way
+        shard = jnp.clip(self.me - step * hop, 0, self.count - 1)
+        ref = self.place(shard, part)
+        return pltpu.make_async_remote_copy(
+            src_ref=ref,
+            dst_ref=ref,
+            send_sem=self.sems.at[0, way, hop, part],
+            recv_sem=self.sems.at[1, way, hop, part],
+            device_id={"row": jnp.clip(self.me + step, 0, self.count - 1)},
+            device_id_type=MESH,
+        )
+
+    def sends(self, way, hop):
+        if way == 0:
+            return (self.me >= hop) & (self.me < self.count - 1)
+        return (self.me + hop < self.count) & (self.me > 0)
+
+    def receives(self, way, hop):
+        if way == 0:
+            return self.me > hop
+        return self.me + hop + 1 < self.count
+
+    def start(self, hop, part):
+        for way in range(2):
+
+            @pl.when(self.sends(way, hop))
+            def _():
+                self.copy(way, hop, part).start()
+
+    def wait(self, way, hop, part):
+        @pl.when(self.receives(way, hop))
+        def _():
+            step = 1 - 2 * way
+            ref = self.place(jnp.clip(self.me - step * (hop + 1), 0, self.count - 1), part)
+            pltpu.make_async_remote_copy(
+                src_ref=ref,
+                dst_ref=ref,
+                send_sem=self.sems.at[0, way, hop, part],
+                recv_sem=self.sems.at[1, way, hop, part],
+                device_id={"row": jnp.clip(self.me - step, 0, self.count - 1)},
+                device_id_type=MESH,
+            ).wait_recv()
+
+    def hand_on(self):
+        for hop in range(self.count - 1):
+
+            def step(part, carry):
+                for way in range(2):
+                    self.wait(way, hop, part)
+                    if hop + 1 < self.count - 1:
+
+                        @pl.when(self.sends(way, hop + 1))
+                        def _():
+                            self.copy(way, hop + 1, part).start()
+
+                return carry
+
+            lax.fori_loop(0, PARTS, step, 0)
+
+    def drain(self):
+        for hop in range(self.count - 1):
+
+            def step(part, carry):
+                for way in range(2):
+
+                    @pl.when(self.sends(way, hop))
+                    def _():
+                        self.copy(way, hop, part).wait_send()
+
+                return carry
+
+            lax.fori_loop(0, PARTS, step, 0)
+
+
+def network(
+    count, picks_ref, features_ref, tiles_ref, bias_ref, out_ref,
+    weights, raw, x_first, x_second, sib_out, sib_in, far_out, far_in, total, turn_out, turn_in,
+    weight_sem, gather_sem, spread_sem, sib_sem, far_sem, turn_sem,
+):
+    layers, pieces, owned, slots, side, _ = weights.shape
+    row, col, rep = (lax.axis_index(name) for name in ("row", "col", "rep"))
+    height = x_first.shape[1]
+    mine = height // count
+    pairs = raw.shape[1]
+    each = owned // PARTS
+    f32, bf16 = jnp.float32, jnp.bfloat16
+
+    def load_weights(layer, piece):
+        return pltpu.make_async_copy(
+            tiles_ref.at[layer, piece], weights.at[layer, piece], weight_sem.at[layer, piece]
+        )
+
+    order = [(1 - col) * 2 + 1 - rep, (1 - col) * 2 + rep, col * 2 + 1 - rep, col * 2 + rep]
     for layer in range(layers):
-        result = relayout(
-            finish(from_rows(result, tiles, tile_rows, tile_counts, layer), bias, layer)
-        )
-    return result
+        for piece in order:
+            load_weights(layer, piece).start()
+
+    barrier = pltpu.get_barrier_semaphore()
+    for away in range(1, count):
+        pl.semaphore_signal(
+            barrier, inc=1, device_id={"row": lax.rem(row + away, count)}, device_id_type=MESH
+        )
+    pl.semaphore_signal(barrier, inc=1, device_id={"rep": 1 - rep}, device_id_type=MESH)
+    pl.semaphore_signal(barrier, inc=1, device_id={"col": 1 - col}, device_id_type=MESH)
+
+    def columns(block):
+        return pl.ds(pl.multiple_of(block * side, side), side)
+
+    def pack(at, carry):
+        low = features_ref[:, columns(at)].astype(f32)
+        high = features_ref[:, columns(at + pairs)].astype(f32)
+        raw[row, at] = jnp.concatenate([low, high], axis=0).astype(bf16)
+        return carry
+
+    lax.fori_loop(0, pairs, pack, 0, unroll=8)
+    pl.semaphore_wait(barrier, count + 1)
+
+    share = pairs // PARTS
+    gather = Chain(count, lambda shard, part: raw.at[shard, pl.ds(part * share, share)], gather_sem)
+    lax.fori_loop(0, PARTS, lambda part, carry: (gather.start(0, part), carry)[1], 0)
+    for x in (x_first, x_second):
+        x[2 * pairs] = jnp.zeros(x.shape[1:], bf16)
+    gather.hand_on()
+
+    def unpack(at, carry):
+        slabs = [raw[shard, at].astype(f32) for shard in range(count)]
+        x_first[at] = jnp.concatenate([s[:mine] for s in slabs], axis=0).astype(bf16)
+        x_first[at + pairs] = jnp.concatenate([s[mine:] for s in slabs], axis=0).astype(bf16)
+        return carry
+
+    lax.fori_loop(0, pairs, unpack, 0, unroll=4)
+
+    spread = Chain(
+        count, lambda shard, part: x_second.at[pl.ds(shard * owned + part * each, each)], spread_sem
+    )
+
+    def sib_copy(layer, which, part):
+        at = pl.ds(part * each, each)
+        return pltpu.make_async_remote_copy(
+            src_ref=sib_out.at[layer, which, at],
+            dst_ref=sib_in.at[layer, which, at],
+            send_sem=sib_sem.at[0, layer, which, part],
+            recv_sem=sib_sem.at[1, layer, which, part],
+            device_id={"rep": 1 - rep},
+            device_id_type=MESH,
+        )
+
+    def far_copy(layer, part):
+        at = pl.ds(part * each, each)
+        return pltpu.make_async_remote_copy(
+            src_ref=far_out.at[layer, at],
+            dst_ref=far_in.at[layer, at],
+            send_sem=far_sem.at[0, layer, part],
+            recv_sem=far_sem.at[1, layer, part],
+            device_id={"col": 1 - col},
+            device_id_type=MESH,
+        )
+
+    def turn_copy(away, part, sender):
+        target = lax.rem(row + away, count)
+        at = pl.ds(part * (each // 2), each // 2)
+        return pltpu.make_async_remote_copy(
+            src_ref=turn_out.at[target, at],
+            dst_ref=turn_in.at[sender, at],
+            send_sem=turn_sem.at[0, away, part],
+            recv_sem=turn_sem.at[1, away, part],
+            device_id={"row": target},
+            device_id_type=MESH,
+        )
+
+    for layer in range(layers):
+        x = x_first if layer == 0 else x_second
+
+        def product(piece, block):
+            first = ((layer * pieces + piece) * owned + block) * slots
+            picked = [x[picks_ref[first + slot]] for slot in range(slots)]
+            tile = weights[layer, piece, block].reshape(slots * side, side)
+            return jnp.dot(jnp.concatenate(picked, axis=1), tile, preferred_element_type=f32)
+
+        def for_sibling(which, piece):
+            load_weights(layer, piece).wait()
+
+            def step(part, carry):
+                for k in range(each):
+                    block = part * each + k
+                    sib_out[layer, which, block] = product(piece, block).astype(bf16)
+                sib_copy(layer, which, part).start()
+                return carry
+
+            lax.fori_loop(0, PARTS, step, 0)
+
+        for_sibling(0, order[0])
+        load_weights(layer, order[1]).wait()
+
+        def for_far(part, carry):
+            sib_copy(layer, 0, part).wait_recv()
+            for k in range(each):
+                block = part * each + k
+                value = product(order[1], block) + sib_in[layer, 0, block].astype(f32)
+                far_out[layer, block] = value.astype(bf16)
+            far_copy(layer, part).start()
+            return carry
+
+        lax.fori_loop(0, PARTS, for_far, 0)
+        for_sibling(1, order[2])
+        load_weights(layer, order[3]).wait()
+
+        def own(part, carry):
+            sib_copy(layer, 1, part).wait_recv()
+            for k in range(each):
+                block = part * each + k
+                total[block] = product(order[3], block) + sib_in[layer, 1, block].astype(f32)
+            return carry
+
+        lax.fori_loop(0, PARTS, own, 0)
+
+        def done(block):
+            shift = bias_ref[layer : layer + 1, columns(row * owned + block)]
+            value = total[block] + far_in[layer, block].astype(f32) + shift
+            return jnp.maximum(value, 0.0)
+
+        def close(part, carry):
+            far_copy(layer, part).wait_recv()
+            if layer + 1 < layers:
+                for k in range(each):
+                    block = part * each + k
+                    x_second[row * owned + block] = done(block).astype(bf16)
+                spread.start(0, part)
+            else:
+                half = each // 2
+                for k in range(half):
+                    at = part * half + k
+                    low, high = done(part * each + k), done(part * each + half + k)
+                    for target in range(count):
+                        rows = slice(target * mine, (target + 1) * mine)
+                        slab = jnp.concatenate([low[rows], high[rows]], axis=0).astype(bf16)
+                        turn_out[target, at] = slab
+                for away in range(1, count):
+                    turn_copy(away, part, row).start()
+            return carry
+
+        lax.fori_loop(0, PARTS, close, 0)
+        if layer + 1 < layers:
+            spread.hand_on()
+
+    def put(sender, source, index, at):
+        half = each // 2
+        slab = source[index, at].astype(f32)
+        block = sender * owned + (at // half) * each + at % half
+        out_ref[:, columns(block)] = slab[:mine].astype(bf16)
+        out_ref[:, columns(block + half)] = slab[mine:].astype(bf16)
+
+    def put_all(sender, source, index):
+        def step(at, carry):
+            put(sender, source, index, at)
+            return carry
+
+        lax.fori_loop(0, owned // 2, step, 0, unroll=4)
+
+    put_all(row, turn_out, row)
+    for away in range(1, count):
+        sender = lax.rem(row + count - away, count)
+        lax.fori_loop(
+            0, PARTS, lambda part, carry: (turn_copy(away, part, sender).wait_recv(), carry)[1], 0
+        )
+        put_all(sender, turn_in, sender)
+
+    def settle(part, carry):
+        for layer in range(layers):
+            far_copy(layer, part).wait_send()
+            for which in range(2):
+                sib_copy(layer, which, part).wait_send()
+        for away in range(1, count):
+            turn_copy(away, part, row).wait_send()
+        return carry
+
+    lax.fori_loop(0, PARTS, settle, 0)
+    gather.drain()
+    spread.drain()
+
+
+def in_kernel(count, features, tiles, tile_rows, tile_counts, bias):
+    layers, pieces, owned, _, slots, side, _ = tiles.shape
+    mine, width = features.shape
+    blocks = width // side
+    height = mine * count
+    live = lax.broadcasted_iota(jnp.int32, tile_rows.shape, 4) < tile_counts[..., None]
+    picks = jnp.where(live, tile_rows, blocks).reshape(-1)
+    bf16, dma = jnp.bfloat16, pltpu.SemaphoreType.DMA
+    return pl.pallas_call(
+        functools.partial(network, count),
+        out_shape=jax.ShapeDtypeStruct((mine, width), bf16),
+        in_specs=[
+            pl.BlockSpec(memory_space=pltpu.SMEM),
+            pl.BlockSpec(memory_space=pltpu.VMEM),
+            pl.BlockSpec(memory_space=pl.ANY),
+            pl.BlockSpec(memory_space=pltpu.VMEM),
+        ],
+        out_specs=pl.BlockSpec(memory_space=pltpu.VMEM),
+        scratch_shapes=[
+            pltpu.VMEM((layers, pieces, owned, slots, side, side), bf16),
+            pltpu.VMEM((count, blocks // 2, 2 * mine, side), bf16),
+            pltpu.VMEM((blocks + 1, height, side), bf16),
+            pltpu.VMEM((blocks + 1, height, side), bf16),
+            pltpu.VMEM((layers, 2, owned, height, side), bf16),
+            pltpu.VMEM((layers, 2, owned, height, side), bf16),
+            pltpu.VMEM((layers, owned, height, side), bf16),
+            pltpu.VMEM((layers, owned, height, side), bf16),
+            pltpu.VMEM((owned, height, side), jnp.float32),
+            pltpu.VMEM((count, owned // 2, 2 * mine, side), bf16),
+            pltpu.VMEM((count, owned // 2, 2 * mine, side), bf16),
+            dma((layers, pieces)),
+            dma((2, 2, count - 1, PARTS)),
+            dma((2, 2, count - 1, PARTS)),
+            dma((2, layers, 2, PARTS)),
+            dma((2, layers, PARTS)),
+            dma((2, count, PARTS)),
+        ],
+        compiler_params=pltpu.CompilerParams(
+            collective_id=0, has_side_effects=True, vmem_limit_bytes=48 * 2**20
+        ),
+        name="network",
+    )(picks, features, tiles.reshape(layers, pieces, owned, slots, side, side), bias)
+
+
+def on_device(sizes, features, tiles, tile_rows, tile_counts, bias):
+    count = sizes["row"]
+    owned = tiles.shape[2]
+    fits = (
+        tiles.shape[0] == 2
+        and sizes["col"] == 2
+        and sizes["rep"] == 2
+        and 1 < count <= 4
+        and features.shape[0] == 8
+        and owned % (2 * PARTS) == 0
+        and 2 * tiles[0].size * 2 <= 32 * 2**20
+    )
+    body = functools.partial(in_kernel, count) if fits else in_operations
+    return body(features, tiles, tile_rows, tile_counts, bias)
 
 
 def solution(mesh):
@@ -62,5 +406,6 @@
     )
     out_specs = P(("grp", "row"), ("col", "rep"))
     return jax.shard_map(
-        on_device, mesh=mesh, in_specs=in_specs, out_specs=out_specs, check_vma=False
-    )
+        functools.partial(on_device, dict(mesh.shape)),
+        mesh=mesh, in_specs=in_specs, out_specs=out_specs, check_vma=False,
+    )

time: 194 us -> 63.1 us (0.33)
  waiting for transfers between devices: 97.8 us -> 0 us
  Pallas kernels: 0 us -> 59.2 us
  local copies, waits for them, and re-layouts: 36.1 us -> 2.89 us
  blocking collectives: 26.6 us -> 0 us
  between operations: 13.3 us -> 0.03 us
  matrix products: 11.8 us -> 0 us
  other arithmetic: 7.77 us -> 0.73 us
    reduce_scatter x2 -> x0, waiting for transfers between devices: 61.9 us -> none  [finish(): lax.psum_scatter(summed, ('col', 'rep'), scatter_dimension=1, tiled=True)]
    pallas_call x0 -> x1, Pallas kernels: none -> 59.2 us  [in_kernel(): pl.pallas_call(functools.partial(network, count), out_shape=jax.ShapeDtyp...]
    all_gather x2 -> x0, waiting for transfers between devices: 35.1 us -> none  [from_rows(): lax.all_gather(current, 'row', axis=0, tiled=True)]
    all_to_all x2 -> x0, blocking collectives: 26.6 us -> none  [relayout(): lax.all_to_all(finished, 'row', split_axis=0, concat_axis=1, tiled=True)]
    slice x6 -> x0, local copies, waits for them, and re-layouts: 22.7 us -> none  [the longest x1 20.9 us: partial_products(): weights = tiles[layer].reshape(out_count, slots, tile_width, tile_width)]
    dot_general x2 -> x0, matrix products: 11.8 us -> none  [partial_products(): jnp.einsum('rosd,osde->roe', picked, weights, preferred_element_type=jnp....]
    gather x2 -> x0, local copies, waits for them, and re-layouts: 6.38 us -> none  [partial_products(): picked = jnp.take(blocks, picks, axis=1)]
    reshape x4 -> x1, local copies, waits for them, and re-layouts: 5.76 us -> 0.2 us  [in_kernel(): picks = jnp.where(live, tile_rows, blocks).reshape(-1)]
  transfers between devices with their start and end apart: 4 -> 0, of which waited for: 4 -> 0; matrix products, arithmetic and copies ran while one was open for 12% -> 0% of each run, Pallas kernels for 0% -> 0%
where the time goes in v1:
time: 63.1 us; the launch traced here: 62.8 us
  Pallas kernels  59.2 us (94%)
  local copies, waits for them, and re-layouts  2.89 us (5%)
  other arithmetic  0.73 us (1%)
    pallas_call x1, Pallas kernels, in_kernel(): pl.pallas_call(functools.partial(network, count), out_shape=jax.ShapeDtyp...  59.2 us
    unnamed x5, local copies, waits for them, and re-layouts  2.55 us

profile of v1, /device:TPU:0, one launch (start us, length us, event | category | flops | bytes accessed | tf_op | source)
XLA Modules:
  0.0 62.8 jit_solution(1066783311889449844)
XLA Ops:
  0.0 0.7 %compare_select_fusion = s32[2,4,32,1,3]{2,3,4,1,0:T(1,128)S(1)} fusion(s32[2,4,32,1,3]{2,3,4,1,0:T(1,128)} %param.7, s32[2,4,32]{2,1,0:T(4,128)} %bitcast.7), kind=kLoop, calls=%fused_computation | loop fusion | flops 1536 | bytes 7168 | tf_op jit(solution)/shard_map/jit(_where)/select_n | solution.py:345
  0.7 0.1 copy.6
  0.9 0.2 reshape.17.picks_ref
  1.1 0.0 copy-start
  1.1 0.9 %copy-done = bf16[8,16384]{1,0:T(8,128)(2,1)S(1)} copy-done((bf16[8,16384]{1,0:T(8,128)(2,1)S(1)}, bf16[8,16384]{1,0:T(8,128)(2,1)}, u32[]{:S(2)}) %copy-start) | copy-done | bytes 262168
  2.0 0.0 copy-start.1
  2.0 0.9 %copy-done.1 = f32[2,16384]{1,0:T(2,128)S(1)} copy-done((f32[2,16384]{1,0:T(2,128)S(1)}, f32[2,16384]{1,0:T(2,128)}, u32[]{:S(2)}) %copy-start.1) | copy-done | bytes 131096
  2.9 59.2 %network.1 = bf16[8,16384]{1,0:T(8,128)(2,1)S(1)} custom-call(s32[768]{0:T(1024)S(1)} %reshape.17.picks_ref, bf16[8,16384]{1,0:T(8,128)(2,1)S(1)} %copy-done, bf16[2,4,32,3,128,128]{5,4,3,2,1,0:T(8,128)(2,1)} %bitcast.6, f32[2,16384]{1,0:T(2,128)S(1)} %copy-done.1), custom_call_target="tpu_custom_call" | custom-call | tf_op jit(solution)/shard_map/network/pallas_call | solution.py:347
  62.1 0.7 %copy.8 = bf16[8,16384]{1,0:T(8,128)(2,1)} copy(bf16[8,16384]{1,0:T(8,128)(2,1)S(1)} %network.1) | data formatting | bytes 524288
Async XLA Ops:
  1.1 1.0 %copy-start = (bf16[8,16384]{1,0:T(8,128)(2,1)S(1)}, bf16[8,16384]{1,0:T(8,128)(2,1)}, u32[]{:S(2)}) copy-start(bf16[8,16384]{1,0:T(8,128)(2,1)} %features_ref.1) | copy-start | bytes 786436
  2.0 0.9 %copy-start.1 = (f32[2,16384]{1,0:T(2,128)S(1)}, f32[2,16384]{1,0:T(2,128)}, u32[]{:S(2)}) copy-start(f32[2,16384]{1,0:T(2,128)} %bias_ref.1) | copy-start | bytes 393220

commit v2 on v0

--- a/solution.py
+++ b/solution.py
@@ -1,7 +1,15 @@
+import functools
+
 import jax
 import jax.numpy as jnp
 from jax import lax
+from jax.experimental import pallas as pl
+from jax.experimental.pallas import tpu as pltpu
 from jax.sharding import PartitionSpec as P
+
+MESH = pl.DeviceIdType.MESH
+PARTS = 4
+CHUNKS = 2
 
 
 def partial_products(rows_x, tiles, tile_rows, tile_counts, layer):
@@ -32,24 +40,392 @@
     return jax.nn.relu(partial_value + shifts[None, :]).astype(jnp.bfloat16)
 
 
-def from_rows(current, tiles, tile_rows, tile_counts, layer):
-    return partial_products(
-        lax.all_gather(current, "row", axis=0, tiled=True), tiles, tile_rows, tile_counts, layer
+def in_operations(features, tiles, tile_rows, tile_counts, bias):
+    layers = tiles.shape[0]
+    rows_x = lax.all_gather(features, "row", axis=0, tiled=True)
+    for layer in range(layers):
+        finished = finish(partial_products(rows_x, tiles, tile_rows, tile_counts, layer), bias, layer)
+        if layer + 1 < layers:
+            rows_x = lax.all_gather(finished, "row", axis=1, tiled=True)
+    return lax.all_to_all(finished, "row", split_axis=0, concat_axis=1, tiled=True)
+
+
+class Line:
+    MOVES = ((2, 2), (3, -2), (0, 1), (1, -1))
+    ON = 4
+
+    def __init__(self, count, place, sems):
+        self.count, self.place, self.sems = count, place, sems
+        self.me = lax.axis_index("row")
+
+    def copy(self, slot, step, shard, part):
+        ref = self.place(jnp.clip(shard, 0, self.count - 1), part)
+        return pltpu.make_async_remote_copy(
+            src_ref=ref,
+            dst_ref=ref,
+            send_sem=self.sems.at[0, slot, part],
+            recv_sem=self.sems.at[1, slot, part],
+            device_id={"row": jnp.clip(self.me + step, 0, self.count - 1)},
+            device_id_type=MESH,
+        )
+
+    def inside(self, step):
+        return self.me < self.count - step if step > 0 else self.me >= -step
+
+    def start(self, part):
+        for slot, step in self.MOVES:
+
+            @pl.when(self.inside(step))
+            def _():
+                self.copy(slot, step, self.me, part).start()
+
+    def hand_on(self, part):
+        for place, slot, step, shard in ((1, 3, -1, 3), (2, 2, 1, 0)):
+
+            @pl.when(self.me == place)
+            def _():
+                self.copy(slot, step, shard, part).wait_recv()
+                self.copy(self.ON, step, shard, part).start()
+
+    def wait(self, part):
+        for slot, step in self.MOVES:
+            came = self.inside(-step)
+            if abs(step) == 2:
+                came = came & ((self.me == 0) | (self.me == self.count - 1))
+
+            @pl.when(came)
+            def _():
+                back = 1 if step < 0 else -1
+                self.copy(slot, back, self.me - step, part).wait_recv()
+
+        for place, step, shard in ((0, 1, 3), (3, -1, 0)):
+
+            @pl.when(self.me == place)
+            def _():
+                self.copy(self.ON, step, shard, part).wait_recv()
+
+    def drain(self, part):
+        for slot, step in self.MOVES:
+
+            @pl.when(self.inside(step))
+            def _():
+                self.copy(slot, step, self.me, part).wait_send()
+
+        for place, step, shard in ((1, -1, 3), (2, 1, 0)):
+
+            @pl.when(self.me == place)
+            def _():
+                self.copy(self.ON, step, shard, part).wait_send()
+
+
+def each_part(body):
+    def step(part, carry):
+        body(part)
+        return carry
+
+    lax.fori_loop(0, PARTS, step, 0)
+
+
+def network(
+    count, picks_ref, features_ref, tiles_ref, bias_ref, out_ref,
+    weights, given, shifts, raw, x_first, x_second_low, x_second_high, sib_out, sib_in, far_out, far_in, total, turn_out, turn_in,
+    weight_sem, load_sem, gather_sem, spread_sem, sib_sem, far_sem, turn_sem,
+):
+    layers, pieces, owned, slots, side, _ = weights.shape
+    row, col, rep = (lax.axis_index(name) for name in ("row", "col", "rep"))
+    chunks, slabs, height = raw.shape[0], raw.shape[2], raw.shape[3]
+    piece_rows = height // count
+    stack = height // piece_rows
+    each = owned // PARTS
+    f32, bf16 = jnp.float32, jnp.bfloat16
+
+    x_second = (x_second_low, x_second_high)
+    take_features = pltpu.make_async_copy(features_ref, given, load_sem.at[0])
+    take_bias = pltpu.make_async_copy(bias_ref, shifts, load_sem.at[1])
+    take_features.start()
+
+    def load_weights(layer, piece):
+        return pltpu.make_async_copy(
+            tiles_ref.at[layer, piece], weights.at[layer, piece], weight_sem.at[layer, piece]
+        )
+
+    barrier = pltpu.get_barrier_semaphore()
+    for away in range(1, count):
+        pl.semaphore_signal(
+            barrier, inc=1, device_id={"row": lax.rem(row + away, count)}, device_id_type=MESH
+        )
+    pl.semaphore_signal(barrier, inc=1, device_id={"rep": 1 - rep}, device_id_type=MESH)
+    pl.semaphore_signal(barrier, inc=1, device_id={"col": 1 - col}, device_id_type=MESH)
+
+    order = [(1 - col) * 2 + 1 - rep, (1 - col) * 2 + rep, col * 2 + 1 - rep, col * 2 + rep]
+    take_features.wait()
+    for layer in range(layers):
+        for piece in order:
+            load_weights(layer, piece).start()
+    take_bias.start()
+
+    def columns(block):
+        return pl.ds(pl.multiple_of(block * side, side), side)
+
+    def pack(at, carry):
+        values = [given[:, columns(at + j * slabs)].astype(f32) for j in range(stack)]
+        for chunk in range(chunks):
+            rows = slice(chunk * piece_rows, (chunk + 1) * piece_rows)
+            raw[chunk, row, at] = jnp.concatenate([v[rows] for v in values], axis=0).astype(bf16)
+        return carry
+
+    lax.fori_loop(0, slabs, pack, 0, unroll=4)
+    pl.semaphore_wait(barrier, count + 1)
+
+    share = slabs // PARTS
+    gathers, spreads = [], []
+    for chunk in range(chunks):
+
+        def raw_place(shard, part, chunk=chunk):
+            return raw.at[chunk, shard, pl.ds(part * share, share)]
+
+        def second_place(shard, part, chunk=chunk):
+            return x_second[chunk].at[pl.ds(shard * owned + part * each, each)]
+
+        gathers.append(Line(count, raw_place, gather_sem.at[chunk]))
+        spreads.append(Line(count, second_place, spread_sem.at[chunk]))
+    for chunk in range(chunks):
+        each_part(gathers[chunk].start)
+    for chunk in range(chunks):
+        for x in (x_first.at[chunk], x_second[chunk]):
+            x[stack * slabs] = jnp.zeros(x.shape[1:], bf16)
+
+    def unpack(chunk):
+        def step(at, carry):
+            values = [raw[chunk, shard, at].astype(f32) for shard in range(count)]
+            for j in range(stack):
+                rows = slice(j * piece_rows, (j + 1) * piece_rows)
+                block = jnp.concatenate([v[rows] for v in values], axis=0).astype(bf16)
+                x_first[chunk, at + j * slabs] = block
+            return carry
+
+        lax.fori_loop(0, slabs, step, 0, unroll=4)
+
+    def sib_copy(layer, chunk, which, part):
+        at = pl.ds(part * each, each)
+        return pltpu.make_async_remote_copy(
+            src_ref=sib_out.at[layer, chunk, which, at],
+            dst_ref=sib_in.at[layer, chunk, which, at],
+            send_sem=sib_sem.at[0, layer, chunk, which, part],
+            recv_sem=sib_sem.at[1, layer, chunk, which, part],
+            device_id={"rep": 1 - rep},
+            device_id_type=MESH,
+        )
+
+    def far_copy(layer, chunk, part):
+        at = pl.ds(part * each, each)
+        return pltpu.make_async_remote_copy(
+            src_ref=far_out.at[layer, chunk, at],
+            dst_ref=far_in.at[layer, chunk, at],
+            send_sem=far_sem.at[0, layer, chunk, part],
+            recv_sem=far_sem.at[1, layer, chunk, part],
+            device_id={"col": 1 - col},
+            device_id_type=MESH,
+        )
+
+    per_part = each // stack
+
+    def turn_copy(chunk, away, part, sender):
+        target = lax.rem(row + away, count)
+        at = pl.ds(part * per_part, per_part)
+        return pltpu.make_async_remote_copy(
+            src_ref=turn_out.at[chunk, target, at],
+            dst_ref=turn_in.at[chunk, sender, at],
+            send_sem=turn_sem.at[0, chunk, away, part],
+            recv_sem=turn_sem.at[1, chunk, away, part],
+            device_id={"row": target},
+            device_id_type=MESH,
+        )
+
+    def run(layer, chunk, beside):
+        x = x_first.at[chunk] if layer == 0 else x_second[chunk]
+
+        def ready(piece):
+            if chunk == 0:
+                load_weights(layer, piece).wait()
+
+        def product(piece, block):
+            first = ((layer * pieces + piece) * owned + block) * slots
+            picked = [x[picks_ref[first + slot]] for slot in range(slots)]
+            tile = weights[layer, piece, block].reshape(slots * side, side)
+            return jnp.dot(jnp.concatenate(picked, axis=1), tile, preferred_element_type=f32)
+
+        def for_sibling(which, piece):
+            ready(piece)
+
+            def step(part):
+                for k in range(each):
+                    block = part * each + k
+                    sib_out[layer, chunk, which, block] = product(piece, block)
+                sib_copy(layer, chunk, which, part).start()
+                if which == 1 and beside is not None:
+                    beside.hand_on(part)
+
+            each_part(step)
+
+        for_sibling(0, order[0])
+        ready(order[1])
+
+        def for_far(part):
+            sib_copy(layer, chunk, 0, part).wait_recv()
+            for k in range(each):
+                block = part * each + k
+                value = product(order[1], block) + sib_in[layer, chunk, 0, block]
+                far_out[layer, chunk, block] = value.astype(bf16)
+            far_copy(layer, chunk, part).start()
+
+        each_part(for_far)
+        for_sibling(1, order[2])
+        ready(order[3])
+
+        def own(part):
+            sib_copy(layer, chunk, 1, part).wait_recv()
+            for k in range(each):
+                block = part * each + k
+                total[block] = product(order[3], block) + sib_in[layer, chunk, 1, block]
+
+        each_part(own)
+
+        def done(block):
+            shift = shifts[layer : layer + 1, columns(row * owned + block)]
+            value = total[block] + far_in[layer, chunk, block].astype(f32) + shift
+            return jnp.maximum(value, 0.0)
+
+        def close(part):
+            far_copy(layer, chunk, part).wait_recv()
+            if layer + 1 < layers:
+                for k in range(each):
+                    block = part * each + k
+                    x_second[chunk][row * owned + block] = done(block).astype(bf16)
+                spreads[chunk].start(part)
+            else:
+                for k in range(per_part):
+                    at = part * per_part + k
+                    values = [done(part * each + j * per_part + k) for j in range(stack)]
+                    for target in range(count):
+                        rows = slice(target * piece_rows, (target + 1) * piece_rows)
+                        slab = jnp.concatenate([v[rows] for v in values], axis=0).astype(bf16)
+                        turn_out[chunk, target, at] = slab
+                for away in range(1, count):
+                    turn_copy(chunk, away, part, row).start()
+
+        each_part(close)
+
+    each_part(gathers[0].hand_on)
+    each_part(gathers[0].wait)
+    unpack(0)
+    take_bias.wait()
+    run(0, 0, gathers[1])
+    each_part(gathers[1].wait)
+    unpack(1)
+    run(0, 1, spreads[0])
+    each_part(spreads[0].wait)
+    run(1, 0, spreads[1])
+    each_part(spreads[1].wait)
+    run(1, 1, None)
+
+    def put_all(sender, source, index):
+        def step(at, carry):
+            values = [source[chunk, index, at].astype(f32) for chunk in range(chunks)]
+            for j in range(stack):
+                rows = slice(j * piece_rows, (j + 1) * piece_rows)
+                block = sender * owned + (at // per_part) * each + j * per_part + at % per_part
+                both = jnp.concatenate([v[rows] for v in values], axis=0)
+                out_ref[:, columns(block)] = both.astype(bf16)
+            return carry
+
+        lax.fori_loop(0, owned // stack, step, 0, unroll=4)
+
+    put_all(row, turn_out, row)
+    for away in range(1, count):
+        sender = lax.rem(row + count - away, count)
+        for chunk in range(chunks):
+            each_part(lambda part: turn_copy(chunk, away, part, sender).wait_recv())
+        put_all(sender, turn_in, sender)
+
+    def settle(part):
+        for chunk in range(chunks):
+            for layer in range(layers):
+                far_copy(layer, chunk, part).wait_send()
+                for which in range(2):
+                    sib_copy(layer, chunk, which, part).wait_send()
+            for away in range(1, count):
+                turn_copy(chunk, away, part, row).wait_send()
+            gathers[chunk].drain(part)
+            spreads[chunk].drain(part)
+
+    each_part(settle)
+
+
+def in_kernel(count, features, tiles, tile_rows, tile_counts, bias):
+    layers, pieces, owned, _, slots, side, _ = tiles.shape
+    mine, width = features.shape
+    blocks = width // side
+    height = mine * count // CHUNKS
+    stack = count
+    live = lax.broadcasted_iota(jnp.int32, tile_rows.shape, 4) < tile_counts[..., None]
+    picks = jnp.where(live, tile_rows, blocks).reshape(-1)
+    f32, bf16, dma = jnp.float32, jnp.bfloat16, pltpu.SemaphoreType.DMA
+    turned = (CHUNKS, count, owned // stack, height, side)
+    return pl.pallas_call(
+        functools.partial(network, count),
+        out_shape=jax.ShapeDtypeStruct((mine, width), bf16),
+        in_specs=[
+            pl.BlockSpec(memory_space=pltpu.SMEM),
+            pl.BlockSpec(memory_space=pl.ANY),
+            pl.BlockSpec(memory_space=pl.ANY),
+            pl.BlockSpec(memory_space=pl.ANY),
+        ],
+        out_specs=pl.BlockSpec(memory_space=pltpu.VMEM),
+        scratch_shapes=[
+            pltpu.VMEM((layers, pieces, owned, slots, side, side), bf16),
+            pltpu.VMEM((mine, width), bf16),
+            pltpu.VMEM(bias.shape, f32),
+            pltpu.VMEM((CHUNKS, count, blocks // stack, height, side), bf16),
+            pltpu.VMEM((CHUNKS, blocks + 1, height, side), bf16),
+            pltpu.VMEM((blocks + 1, height, side), bf16),
+            pltpu.VMEM((blocks + 1, height, side), bf16),
+            pltpu.VMEM((layers, CHUNKS, 2, owned, height, side), f32),
+            pltpu.VMEM((layers, CHUNKS, 2, owned, height, side), f32),
+            pltpu.VMEM((layers, CHUNKS, owned, height, side), bf16),
+            pltpu.VMEM((layers, CHUNKS, owned, height, side), bf16),
+            pltpu.VMEM((owned, height, side), f32),
+            pltpu.VMEM(turned, bf16),
+            pltpu.VMEM(turned, bf16),
+            dma((layers, pieces)),
+            dma((2,)),
+            dma((CHUNKS, 2, 5, PARTS)),
+            dma((CHUNKS, 2, 5, PARTS)),
+            dma((2, layers, CHUNKS, 2, PARTS)),
+            dma((2, layers, CHUNKS, PARTS)),
+            dma((2, CHUNKS, count, PARTS)),
+        ],
+        compiler_params=pltpu.CompilerParams(
+            collective_id=0, has_side_effects=True, vmem_limit_bytes=56 * 2**20
+        ),
+        name="network",
+    )(picks, features, tiles.reshape(layers, pieces, owned, slots, side, side), bias)
+
+
+def on_device(sizes, features, tiles, tile_rows, tile_counts, bias):
+    count = sizes["row"]
+    owned = tiles.shape[2]
+    fits = (
+        tiles.shape[0] == 2
+        and sizes["col"] == 2
+        and sizes["rep"] == 2
+        and count == 4
+        and features.shape[0] == 8
+        and owned % (4 * PARTS) == 0
+        and 2 * tiles[0].size * 2 <= 32 * 2**20
     )
-
-
-def relayout(finished):
-    return lax.all_to_all(finished, "row", split_axis=0, concat_axis=1, tiled=True)
-
-
-def on_device(features, tiles, tile_rows, tile_counts, bias):
-    layers = tiles.shape[0]
-    result = features
-    for layer in range(layers):
-        result = relayout(
-            finish(from_rows(result, tiles, tile_rows, tile_counts, layer), bias, layer)
-        )
-    return result
+    body = functools.partial(in_kernel, count) if fits else in_operations
+    return body(features, tiles, tile_rows, tile_counts, bias)
 
 
 def solution(mesh):
@@ -62,5 +438,6 @@
     )
     out_specs = P(("grp", "row"), ("col", "rep"))
     return jax.shard_map(
-        on_device, mesh=mesh, in_specs=in_specs, out_specs=out_specs, check_vma=False
+        functools.partial(on_device, dict(mesh.shape)),
+        mesh=mesh, in_specs=in_specs, out_specs=out_specs, check_vma=False,
     )

time: 194 us -> 63 us (0.32)
  waiting for transfers between devices: 97.8 us -> 0 us
  Pallas kernels: 0 us -> 59.4 us
  local copies, waits for them, and re-layouts: 36.1 us -> 2.6 us
  blocking collectives: 26.6 us -> 0 us
  between operations: 13.3 us -> 0.01 us
  matrix products: 11.8 us -> 0 us
  other arithmetic: 7.77 us -> 0.73 us
    reduce_scatter x2 -> x0, waiting for transfers between devices: 61.9 us -> none  [finish(): lax.psum_scatter(summed, ('col', 'rep'), scatter_dimension=1, tiled=True)]
    pallas_call x0 -> x1, Pallas kernels: none -> 59.4 us  [in_kernel(): pl.pallas_call(functools.partial(network, count), out_shape=jax.ShapeDtyp...]
    all_gather x2 -> x0, waiting for transfers between devices: 35.1 us -> none  [from_rows(): lax.all_gather(current, 'row', axis=0, tiled=True)]
    all_to_all x2 -> x0, blocking collectives: 26.6 us -> none  [relayout(): lax.all_to_all(finished, 'row', split_axis=0, concat_axis=1, tiled=True)]
    slice x6 -> x0, local copies, waits for them, and re-layouts: 22.7 us -> none  [the longest x1 20.9 us: partial_products(): weights = tiles[layer].reshape(out_count, slots, tile_width, tile_width)]
    dot_general x2 -> x0, matrix products: 11.8 us -> none  [partial_products(): jnp.einsum('rosd,osde->roe', picked, weights, preferred_element_type=jnp....]
    gather x2 -> x0, local copies, waits for them, and re-layouts: 6.38 us -> none  [partial_products(): picked = jnp.take(blocks, picks, axis=1)]
    reshape x4 -> x1, local copies, waits for them, and re-layouts: 5.76 us -> 0.8 us  [in_kernel(): picks = jnp.where(live, tile_rows, blocks).reshape(-1)]
  transfers between devices with their start and end apart: 4 -> 0, of which waited for: 4 -> 0; matrix products, arithmetic and copies ran while one was open for 12% -> 0% of each run, Pallas kernels for 0% -> 0%
where the time goes in v2:
time: 63 us; the launch traced here: 62.7 us
  Pallas kernels  59.4 us (94%)
  local copies, waits for them, and re-layouts  2.6 us (4%)
  other arithmetic  0.73 us (1%)
    pallas_call x1, Pallas kernels, in_kernel(): pl.pallas_call(functools.partial(network, count), out_shape=jax.ShapeDtyp...  59.4 us
    unnamed x1, local copies, waits for them, and re-layouts  1.67 us

profile of v2, /device:TPU:0, one launch (start us, length us, event | category | flops | bytes accessed | tf_op | source)
XLA Modules:
  0.0 62.7 jit_solution(2474282538969454046)
XLA Ops:
  0.0 0.7 %compare_select_fusion = s32[2,4,32,1,3]{2,3,4,1,0:T(1,128)S(1)} fusion(s32[2,4,32,1,3]{2,3,4,1,0:T(1,128)} %param.7, s32[2,4,32]{2,1,0:T(4,128)} %bitcast.7), kind=kLoop, calls=%fused_computation | loop fusion | flops 1536 | bytes 7168 | tf_op jit(solution)/shard_map/jit(_where)/select_n | solution.py:372
  0.7 0.1 copy.6
  0.9 0.8 %reshape.17.picks_ref = s32[768]{0:T(1024)} reshape(s32[2,4,32,1,3]{4,2,1,0,3:T(8,128)S(1)} %copy.6) | data formatting | bytes 6144 | tf_op jit(solution)/shard_map/reshape | solution.py:372
  1.7 59.4 %network.1 = bf16[8,16384]{1,0:T(8,128)(2,1)} custom-call(s32[768]{0:T(1024)} %reshape.17.picks_ref, bf16[8,16384]{1,0:T(8,128)(2,1)} %features_ref.1, bf16[2,4,32,3,128,128]{5,4,3,2,1,0:T(8,128)(2,1)} %bitcast.6, f32[2,16384]{1,0:T(2,128)} %bias_ref.1), custom_call_target="tpu_custom_call" | custom-call | tf_op jit(solution)/shard_map/network/pallas_call | solution.py:375
  61.1 1.7 %copy.8 = bf16[8,16384]{1,0:T(8,128)(2,1)} copy(bf16[8,16384]{1,0:T(8,128)(2,1)} %network.1) | data formatting | bytes 524288

commit v3 on v2

--- a/solution.py
+++ b/solution.py
@@ -60,11 +60,12 @@
 
     def copy(self, slot, step, shard, part):
         ref = self.place(jnp.clip(shard, 0, self.count - 1), part)
+        own = part if slot in (2, 3) and part is not None else 0
         return pltpu.make_async_remote_copy(
             src_ref=ref,
             dst_ref=ref,
-            send_sem=self.sems.at[0, slot, part],
-            recv_sem=self.sems.at[1, slot, part],
+            send_sem=self.sems.at[0, slot, 0],
+            recv_sem=self.sems.at[1, slot, own],
             device_id={"row": jnp.clip(self.me + step, 0, self.count - 1)},
             device_id_type=MESH,
         )
@@ -87,7 +88,7 @@
                 self.copy(slot, step, shard, part).wait_recv()
                 self.copy(self.ON, step, shard, part).start()
 
-    def wait(self, part):
+    def wait(self):
         for slot, step in self.MOVES:
             came = self.inside(-step)
             if abs(step) == 2:
@@ -96,26 +97,29 @@
             @pl.when(came)
             def _():
                 back = 1 if step < 0 else -1
-                self.copy(slot, back, self.me - step, part).wait_recv()
+                if abs(step) == 2:
+                    each_part(lambda part: self.copy(slot, back, self.me - step, part).wait_recv())
+                else:
+                    self.copy(slot, back, self.me - step, None).wait_recv()
 
         for place, step, shard in ((0, 1, 3), (3, -1, 0)):
 
             @pl.when(self.me == place)
             def _():
-                self.copy(self.ON, step, shard, part).wait_recv()
-
-    def drain(self, part):
+                self.copy(self.ON, step, shard, None).wait_recv()
+
+    def drain(self):
         for slot, step in self.MOVES:
 
             @pl.when(self.inside(step))
             def _():
-                self.copy(slot, step, self.me, part).wait_send()
+                self.copy(slot, step, self.me, None).wait_send()
 
         for place, step, shard in ((1, -1, 3), (2, 1, 0)):
 
             @pl.when(self.me == place)
             def _():
-                self.copy(self.ON, step, shard, part).wait_send()
+                self.copy(self.ON, step, shard, None).wait_send()
 
 
 def each_part(body):
@@ -177,15 +181,18 @@
     lax.fori_loop(0, slabs, pack, 0, unroll=4)
     pl.semaphore_wait(barrier, count + 1)
 
+    def some(part, size, whole, base=0):
+        return pl.ds(base, whole) if part is None else pl.ds(base + part * size, size)
+
     share = slabs // PARTS
     gathers, spreads = [], []
     for chunk in range(chunks):
 
         def raw_place(shard, part, chunk=chunk):
-            return raw.at[chunk, shard, pl.ds(part * share, share)]
+            return raw.at[chunk, shard, some(part, share, slabs)]
 
         def second_place(shard, part, chunk=chunk):
-            return x_second[chunk].at[pl.ds(shard * owned + part * each, each)]
+            return x_second[chunk].at[some(part, each, owned, shard * owned)]
 
         gathers.append(Line(count, raw_place, gather_sem.at[chunk]))
         spreads.append(Line(count, second_place, spread_sem.at[chunk]))
@@ -207,23 +214,23 @@
         lax.fori_loop(0, slabs, step, 0, unroll=4)
 
     def sib_copy(layer, chunk, which, part):
-        at = pl.ds(part * each, each)
+        at = some(part, each, owned)
         return pltpu.make_async_remote_copy(
             src_ref=sib_out.at[layer, chunk, which, at],
             dst_ref=sib_in.at[layer, chunk, which, at],
-            send_sem=sib_sem.at[0, layer, chunk, which, part],
-            recv_sem=sib_sem.at[1, layer, chunk, which, part],
+            send_sem=sib_sem.at[0, layer, chunk, which, 0],
+            recv_sem=sib_sem.at[1, layer, chunk, which, 0 if part is None else part],
             device_id={"rep": 1 - rep},
             device_id_type=MESH,
         )
 
     def far_copy(layer, chunk, part):
-        at = pl.ds(part * each, each)
+        at = some(part, each, owned)
         return pltpu.make_async_remote_copy(
             src_ref=far_out.at[layer, chunk, at],
             dst_ref=far_in.at[layer, chunk, at],
-            send_sem=far_sem.at[0, layer, chunk, part],
-            recv_sem=far_sem.at[1, layer, chunk, part],
+            send_sem=far_sem.at[0, layer, chunk, 0],
+            recv_sem=far_sem.at[1, layer, chunk, 0 if part is None else part],
             device_id={"col": 1 - col},
             device_id_type=MESH,
         )
@@ -232,12 +239,12 @@
 
     def turn_copy(chunk, away, part, sender):
         target = lax.rem(row + away, count)
-        at = pl.ds(part * per_part, per_part)
+        at = some(part, per_part, owned // stack)
         return pltpu.make_async_remote_copy(
             src_ref=turn_out.at[chunk, target, at],
             dst_ref=turn_in.at[chunk, sender, at],
-            send_sem=turn_sem.at[0, chunk, away, part],
-            recv_sem=turn_sem.at[1, chunk, away, part],
+            send_sem=turn_sem.at[0, chunk, away],
+            recv_sem=turn_sem.at[1, chunk, away],
             device_id={"row": target},
             device_id_type=MESH,
         )
@@ -316,18 +323,32 @@
 
         each_part(close)
 
+    def settle(layer, chunk):
+        far_copy(layer, chunk, None).wait_send()
+        for which in range(2):
+            sib_copy(layer, chunk, which, None).wait_send()
+        if layer + 1 == layers:
+            for away in range(1, count):
+                turn_copy(chunk, away, None, row).wait_send()
+
     each_part(gathers[0].hand_on)
-    each_part(gathers[0].wait)
+    gathers[0].wait()
     unpack(0)
     take_bias.wait()
     run(0, 0, gathers[1])
-    each_part(gathers[1].wait)
+    gathers[1].wait()
     unpack(1)
     run(0, 1, spreads[0])
-    each_part(spreads[0].wait)
+    spreads[0].wait()
     run(1, 0, spreads[1])
-    each_part(spreads[1].wait)
+    for chunk in range(chunks):
+        gathers[chunk].drain()
+        settle(0, chunk)
+    settle(1, 0)
+    spreads[0].drain()
+    spreads[1].wait()
     run(1, 1, None)
+    spreads[1].drain()
 
     def put_all(sender, source, index):
         def step(at, carry):
@@ -345,21 +366,9 @@
     for away in range(1, count):
         sender = lax.rem(row + count - away, count)
         for chunk in range(chunks):
-            each_part(lambda part: turn_copy(chunk, away, part, sender).wait_recv())
+            turn_copy(chunk, away, None, sender).wait_recv()
         put_all(sender, turn_in, sender)
-
-    def settle(part):
-        for chunk in range(chunks):
-            for layer in range(layers):
-                far_copy(layer, chunk, part).wait_send()
-                for which in range(2):
-                    sib_copy(layer, chunk, which, part).wait_send()
-            for away in range(1, count):
-                turn_copy(chunk, away, part, row).wait_send()
-            gathers[chunk].drain(part)
-            spreads[chunk].drain(part)
-
-    each_part(settle)
+    settle(1, 1)
 
 
 def in_kernel(count, features, tiles, tile_rows, tile_counts, bias):
@@ -403,7 +412,7 @@
             dma((CHUNKS, 2, 5, PARTS)),
             dma((2, layers, CHUNKS, 2, PARTS)),
             dma((2, layers, CHUNKS, PARTS)),
-            dma((2, CHUNKS, count, PARTS)),
+            dma((2, CHUNKS, count)),
         ],
         compiler_params=pltpu.CompilerParams(
             collective_id=0, has_side_effects=True, vmem_limit_bytes=56 * 2**20

time: 63 us -> 62.4 us (level)
  Pallas kernels: 59.4 us -> 58.7 us
    pallas_call x1, Pallas kernels: 59.4 us -> 58.7 us  [in_kernel(): pl.pallas_call(functools.partial(network, count), out_shape=jax.ShapeDtyp...]
where the time goes in v3:
time: 62.4 us; the launch traced here: 62.1 us
  Pallas kernels  58.7 us (94%)
  local copies, waits for them, and re-layouts  2.6 us (4%)
  other arithmetic  0.73 us (1%)
    pallas_call x1, Pallas kernels, in_kernel(): pl.pallas_call(functools.partial(network, count), out_shape=jax.ShapeDtyp...  58.7 us
    unnamed x1, local copies, waits for them, and re-layouts  1.67 us

profile of v3, /device:TPU:0, one launch (start us, length us, event | category | flops | bytes accessed | tf_op | source)
XLA Modules:
  0.0 62.1 jit_solution(9173931365307576175)
XLA Ops:
  0.0 0.7 %compare_select_fusion = s32[2,4,32,1,3]{2,3,4,1,0:T(1,128)S(1)} fusion(s32[2,4,32,1,3]{2,3,4,1,0:T(1,128)} %param.7, s32[2,4,32]{2,1,0:T(4,128)} %bitcast.7), kind=kLoop, calls=%fused_computation | loop fusion | flops 1536 | bytes 7168 | tf_op jit(solution)/shard_map/jit(_where)/select_n | solution.py:381
  0.7 0.1 copy.6
  0.9 0.8 %reshape.17.picks_ref = s32[768]{0:T(1024)} reshape(s32[2,4,32,1,3]{4,2,1,0,3:T(8,128)S(1)} %copy.6) | data formatting | bytes 6144 | tf_op jit(solution)/shard_map/reshape | solution.py:381
  1.7 58.7 %network.1 = bf16[8,16384]{1,0:T(8,128)(2,1)} custom-call(s32[768]{0:T(1024)} %reshape.17.picks_ref, bf16[8,16384]{1,0:T(8,128)(2,1)} %features_ref.1, bf16[2,4,32,3,128,128]{5,4,3,2,1,0:T(8,128)(2,1)} %bitcast.6, f32[2,16384]{1,0:T(2,128)} %bias_ref.1), custom_call_target="tpu_custom_call" | custom-call | tf_op jit(solution)/shard_map/network/pallas_call | solution.py:384
  60.4 1.7 %copy.8 = bf16[8,16384]{1,0:T(8,128)(2,1)} copy(bf16[8,16384]{1,0:T(8,128)(2,1)} %network.1) | data formatting | bytes 524288

commit v4 on v3

--- a/solution.py
+++ b/solution.py
@@ -8,7 +8,7 @@
 from jax.sharding import PartitionSpec as P
 
 MESH = pl.DeviceIdType.MESH
-PARTS = 4
+PARTS = 2
 CHUNKS = 2
 
 
@@ -171,14 +171,17 @@
     def columns(block):
         return pl.ds(pl.multiple_of(block * side, side), side)
 
-    def pack(at, carry):
-        values = [given[:, columns(at + j * slabs)].astype(f32) for j in range(stack)]
-        for chunk in range(chunks):
-            rows = slice(chunk * piece_rows, (chunk + 1) * piece_rows)
+    def pack(chunk):
+        rows = slice(chunk * piece_rows, (chunk + 1) * piece_rows)
+
+        def step(at, carry):
+            values = [given[:, columns(at + j * slabs)].astype(f32) for j in range(stack)]
             raw[chunk, row, at] = jnp.concatenate([v[rows] for v in values], axis=0).astype(bf16)
-        return carry
-
-    lax.fori_loop(0, slabs, pack, 0, unroll=4)
+            return carry
+
+        lax.fori_loop(0, slabs, step, 0, unroll=4)
+
+    pack(0)
     pl.semaphore_wait(barrier, count + 1)
 
     def some(part, size, whole, base=0):
@@ -196,7 +199,9 @@
 
         gathers.append(Line(count, raw_place, gather_sem.at[chunk]))
         spreads.append(Line(count, second_place, spread_sem.at[chunk]))
-    for chunk in range(chunks):
+    each_part(gathers[0].start)
+    for chunk in range(1, chunks):
+        pack(chunk)
         each_part(gathers[chunk].start)
     for chunk in range(chunks):
         for x in (x_first.at[chunk], x_second[chunk]):
@@ -270,8 +275,6 @@
                     block = part * each + k
                     sib_out[layer, chunk, which, block] = product(piece, block)
                 sib_copy(layer, chunk, which, part).start()
-                if which == 1 and beside is not None:
-                    beside.hand_on(part)
 
             each_part(step)
 
@@ -285,6 +288,8 @@
                 value = product(order[1], block) + sib_in[layer, chunk, 0, block]
                 far_out[layer, chunk, block] = value.astype(bf16)
             far_copy(layer, chunk, part).start()
+            if beside is not None:
+                beside.hand_on(part)
 
         each_part(for_far)
         for_sibling(1, order[2])
@@ -415,7 +420,7 @@
             dma((2, CHUNKS, count)),
         ],
         compiler_params=pltpu.CompilerParams(
-            collective_id=0, has_side_effects=True, vmem_limit_bytes=56 * 2**20
+            collective_id=0, has_side_effects=True, vmem_limit_bytes=40 * 2**20
         ),
         name="network",
     )(picks, features, tiles.reshape(layers, pieces, owned, slots, side, side), bias)

time: 62.4 us -> 61 us (0.978)
  Pallas kernels: 58.7 us -> 57.1 us
    pallas_call x1, Pallas kernels: 58.7 us -> 57.1 us  [in_kernel(): pl.pallas_call(functools.partial(network, count), out_shape=jax.ShapeDtyp...]
    unnamed x1 -> x5, local copies, waits for them, and re-layouts: 1.67 us -> 2.55 us
where the time goes in v4:
time: 61 us; the launch traced here: 60.8 us
  Pallas kernels  57.1 us (94%)
  local copies, waits for them, and re-layouts  2.89 us (5%)
  other arithmetic  0.73 us (1%)
    pallas_call x1, Pallas kernels, in_kernel(): pl.pallas_call(functools.partial(network, count), out_shape=jax.ShapeDtyp...  57.1 us
    unnamed x5, local copies, waits for them, and re-layouts  2.55 us

profile of v4, /device:TPU:0, one launch (start us, length us, event | category | flops | bytes accessed | tf_op | source)
XLA Modules:
  0.0 60.8 jit_solution(5275047375607384540)
XLA Ops:
  0.0 0.7 %compare_select_fusion = s32[2,4,32,1,3]{2,3,4,1,0:T(1,128)S(1)} fusion(s32[2,4,32,1,3]{2,3,4,1,0:T(1,128)} %param.7, s32[2,4,32]{2,1,0:T(4,128)} %bitcast.7), kind=kLoop, calls=%fused_computation | loop fusion | flops 1536 | bytes 7168 | tf_op jit(solution)/shard_map/jit(_where)/select_n | solution.py:386
  0.7 0.1 copy.6
  0.9 0.2 reshape.17.picks_ref
  1.1 0.0 copy-start
  1.1 0.9 %copy-done = bf16[8,16384]{1,0:T(8,128)(2,1)S(1)} copy-done((bf16[8,16384]{1,0:T(8,128)(2,1)S(1)}, bf16[8,16384]{1,0:T(8,128)(2,1)}, u32[]{:S(2)}) %copy-start) | copy-done | bytes 262168
  2.0 0.0 copy-start.1
  2.0 0.9 %copy-done.1 = f32[2,16384]{1,0:T(2,128)S(1)} copy-done((f32[2,16384]{1,0:T(2,128)S(1)}, f32[2,16384]{1,0:T(2,128)}, u32[]{:S(2)}) %copy-start.1) | copy-done | bytes 131096
  2.9 57.1 %network.1 = bf16[8,16384]{1,0:T(8,128)(2,1)S(1)} custom-call(s32[768]{0:T(1024)S(1)} %reshape.17.picks_ref, bf16[8,16384]{1,0:T(8,128)(2,1)S(1)} %copy-done, bf16[2,4,32,3,128,128]{5,4,3,2,1,0:T(8,128)(2,1)} %bitcast.6, f32[2,16384]{1,0:T(2,128)S(1)} %copy-done.1), custom_call_target="tpu_custom_call" | custom-call | tf_op jit(solution)/shard_map/network/pallas_call | solution.py:389
  60.1 0.7 %copy.8 = bf16[8,16384]{1,0:T(8,128)(2,1)} copy(bf16[8,16384]{1,0:T(8,128)(2,1)S(1)} %network.1) | data formatting | bytes 524288
Async XLA Ops:
  1.1 1.0 %copy-start = (bf16[8,16384]{1,0:T(8,128)(2,1)S(1)}, bf16[8,16384]{1,0:T(8,128)(2,1)}, u32[]{:S(2)}) copy-start(bf16[8,16384]{1,0:T(8,128)(2,1)} %features_ref.1) | copy-start | bytes 786436
  2.0 0.9 %copy-start.1 = (f32[2,16384]{1,0:T(2,128)S(1)}, f32[2,16384]{1,0:T(2,128)}, u32[]{:S(2)}) copy-start(f32[2,16384]{1,0:T(2,128)} %bias_ref.1) | copy-start | bytes 393220
